TPU v7x, 512 devices: a whole 4x4x16 slice. The times are simulated.
512 devices in a mesh: fsdp: 16 (over z_hi, y, core), chan: 32 (over z_lo, x).
Axes of the slice: x: 4, y: 4, z: 16 (z_hi: 2, z_lo: 8; z = z_hi * 8 + z_lo), core: 2. Of those that a mesh axis runs over, the one named last changes fastest.
Arguments:
- xs_in: bfloat16 [8192, 16384], P('fsdp', 'chan'), may hold values from -6 to 6
- gate_in: bfloat16 [8192, 16384], P('fsdp', 'chan'), may hold values from -110 to 110
- bc_in: bfloat16 [8192, 4096], P('fsdp', 'chan'), may hold values from -6 to 6
- dt_raw: float32 [8192, 256], P('fsdp', 'chan'), may hold values from -7.8 to 1.8
- x_tail: bfloat16 [32, 3, 16384], P('fsdp', None, 'chan'), may hold values from -6 to 6
- bc_tail: bfloat16 [32, 3, 4096], P('fsdp', None, 'chan'), may hold values from -6 to 6
- conv_x_w: float32 [4, 16384], P(None, 'chan'), may hold values from -3 to 3
- conv_x_b: float32 [16384], P('chan'), may hold values from -2 to 2
- conv_bc_w: float32 [4, 4096], P(None, 'chan'), may hold values from -3 to 3
- conv_bc_b: float32 [4096], P('chan'), may hold values from -2 to 2
- dt_bias: float32 [256], P('chan'), may hold values from -1 to 0.5
- a_log: float32 [256], P('chan'), may hold values from -1.9 to 1.6
- skip_d: float32 [256], P('chan'), may hold values from 0.5 to 1.5
- state_in: float32 [32, 256, 64, 256], P('fsdp', 'chan'), may hold values from -0.5 to 0.5
- norm_gain: float32 [16384], P('chan'), may hold values from 0.1 to 1.9
- out_values: bfloat16 [16384, 4096], P('chan', 'fsdp'), may hold values from -0.09375 to 0.09375
- out_scales: float32 [128, 32], P('chan', 'fsdp'), may hold values from 0.5 to 2
Outputs:
- mixed_out: bfloat16 [8192, 4096], P('fsdp', 'chan')
- new_state: float32 [32, 256, 64, 256], P('fsdp', 'chan')
All inputs are finite; a program needn't handle non-finite values.
Results may differ from a plain program's by a relative error of at most 0.03.
Values may be sent and summed in bfloat16 or wider, within the bound.
A program may use at most 64 MiB of HBM per device.

v0:
```python
import jax
import jax.numpy as jnp
from jax import lax
from jax.sharding import PartitionSpec as P

BLOCK = 128


EPS = 1e-05


def partner_2(shard, axis, stride):
    return lax.ppermute(shard, axis, [(i, i ^ 1 << stride) for i in range(lax.axis_size(axis))])


def causal_conv(inputs, prefix, weight, offset):
    padded = jnp.concatenate([prefix, inputs], axis=1).astype(jnp.float32)
    length = inputs.shape[1]
    tap_count = weight.shape[0]
    running = offset[None, None, :] + weight[0][None, None, :] * padded[:, 0:length]
    for tap_index in range(1, tap_count):
        running = (
            running + weight[tap_index][None, None, :] * padded[:, tap_index : tap_index + length]
        )
    return jax.nn.silu(running).astype(jnp.bfloat16)


def span_scan(x_heads, b_state, c_state, step_size, decay_rate, skip_gain, carried):
    length = step_size.shape[0]
    highest = lax.Precision.HIGHEST
    scores = jnp.einsum("tn,sn->ts", c_state, b_state, preferred_element_type=jnp.float32)
    log_decay = jnp.cumsum(-decay_rate[None, :] * step_size, axis=0)
    by_head = log_decay.T
    spread = by_head[:, :, None] - by_head[:, None, :]
    row_ids = lax.broadcasted_iota(jnp.int32, (length, length), 0)
    col_ids = lax.broadcasted_iota(jnp.int32, (length, length), 1)
    causal = (row_ids >= col_ids)[None]
    decay = jnp.where(causal, jnp.exp(jnp.where(causal, spread, 0.0)), 0.0)
    mixing = (scores[None] * decay * step_size.T[:, None, :]).astype(jnp.bfloat16)
    within = jnp.einsum("hts,shp->thp", mixing, x_heads, preferred_element_type=jnp.float32)
    from_state = jnp.einsum("tn,hpn->thp", c_state.astype(jnp.float32), carried, precision=highest)
    from_state = from_state * jnp.exp(log_decay)[:, :, None]
    outputs = within + from_state + skip_gain[None, :, None] * x_heads.astype(jnp.float32)
    final_log = log_decay[-1]
    weighting = jnp.exp(final_log[None, :] - log_decay) * step_size
    weighted = x_heads.astype(jnp.float32) * weighting[:, :, None]
    updated = jnp.exp(final_log)[:, None, None] * carried + jnp.einsum(
        "shp,sn->hpn", weighted, b_state.astype(jnp.float32), precision=highest
    )
    return (outputs, updated)


def per_device(
    xs_in,
    gate_in,
    bc_in,
    dt_raw,
    x_tail,
    bc_tail,
    conv_x_w,
    conv_x_b,
    conv_bc_w,
    conv_bc_b,
    dt_bias,
    a_log,
    skip_d,
    state_in,
    norm_gain,
    out_values,
    out_scales,
):
    chan_index = lax.axis_index("chan")
    request_count = state_in.shape[0]
    length = xs_in.shape[0] // request_count
    head_dev = dt_raw.shape[1]
    head_width = state_in.shape[2]
    state_width = state_in.shape[3]
    inner_dev = head_dev * head_width
    token_rows = request_count * length
    x_conv = causal_conv(
        xs_in.reshape(request_count, length, inner_dev), x_tail, conv_x_w, conv_x_b
    )
    bc_conv = causal_conv(
        bc_in.reshape(request_count, length, -1), bc_tail, conv_bc_w, conv_bc_b
    ).reshape(token_rows, -1)
    quarter = bc_conv.shape[1]
    group_bc = bc_conv
    for bit_index in range(2):
        partner = partner_2(group_bc, "chan", bit_index)
        is_upper = chan_index // (1 << bit_index) % 2 == 1
        group_bc = jnp.where(
            is_upper,
            jnp.concatenate([partner, group_bc], axis=1),
            jnp.concatenate([group_bc, partner], axis=1),
        )
    group_bc = group_bc.reshape(request_count, length, 4 * quarter)
    step_size = jax.nn.softplus(dt_raw + dt_bias[None, :]).reshape(request_count, length, head_dev)
    decay_rate = jnp.exp(a_log)

    def one_request(x_rows, bc_rows, step_rows, carried):
        return span_scan(
            x_rows.reshape(length, head_dev, head_width),
            bc_rows[:, :state_width],
            bc_rows[:, state_width:],
            step_rows,
            decay_rate,
            skip_d,
            carried,
        )

    ssd_out, new_state = jax.vmap(one_request)(x_conv, group_bc, step_size, state_in)
    gated = ssd_out.reshape(token_rows, inner_dev) * jax.nn.silu(gate_in.astype(jnp.float32))
    summed_sq = jnp.sum(gated * gated, axis=1)[None, :]
    for bit_index in range(2):
        summed_sq = summed_sq + partner_2(summed_sq, "chan", bit_index)
    group_sq = summed_sq[0]
    mean_sq = group_sq / (4 * inner_dev)
    hidden = (gated * lax.rsqrt(mean_sq + EPS)[:, None] * norm_gain[None, :]).astype(jnp.bfloat16)
    scales = jnp.repeat(jnp.repeat(out_scales, BLOCK, axis=0), BLOCK, axis=1)
    weight_local = (out_values.astype(jnp.float32) * scales).astype(jnp.bfloat16)
    partial_out = jnp.dot(
        hidden,
        lax.all_gather(weight_local, "fsdp", axis=1, tiled=True),
        preferred_element_type=jnp.float32,
    )
    mixed_out = lax.psum_scatter(
        partial_out.astype(jnp.bfloat16), "chan", scatter_dimension=1, tiled=True
    )
    return (mixed_out, new_state)


def solution(mesh):
    placed = (
        P("fsdp", "chan"),
        P("fsdp", "chan"),
        P("fsdp", "chan"),
        P("fsdp", "chan"),
        P("fsdp", None, "chan"),
        P("fsdp", None, "chan"),
        P(None, "chan"),
        P("chan"),
        P(None, "chan"),
        P("chan"),
        P("chan"),
        P("chan"),
        P("chan"),
        P("fsdp", "chan", None, None),
        P("chan"),
        P("chan", "fsdp"),
        P("chan", "fsdp"),
    )
    return jax.shard_map(
        per_device,
        mesh=mesh,
        in_specs=placed,
        out_specs=(P("fsdp", "chan"), P("fsdp", "chan", None, None)),
        check_vma=False,
    )
```

profile of v0, /device:TPU:8, one launch (start us, length us, event | category | flops | bytes accessed | tf_op | source)
XLA Modules:
  0.0 398.7 jit_solution(6106257406891268573)
XLA Ops:
  7.2 0.0 all-gather.2.cloned.1.call-start
  7.2 0.8 copy.45
  8.1 0.6 broadcast_in_dim.47
  8.7 1.7 fusion.18
  10.4 0.0 all-gather.2.cloned.1.call-update
  10.4 0.0 reduce-scatter.4.cloned.1.call-start
  10.5 0.7 copy.42
  11.1 0.9 maximum_convert_fusion.1
  12.1 0.8 slice_bitcast_fusion.3
  12.9 0.8 multiply_convert_fusion.7
  13.8 3.4 collective-permute-start
  17.2 0.7 exponential_negate_fusion
  17.8 0.8 compare_select_fusion
  18.7 0.1 multiply_bitcast_fusion
  18.7 1.1 reduce-window.6
  19.9 0.2 slice_reduce_fusion
  20.1 0.9 copy.40
  21.0 0.0 copy-start.3
  21.0 0.2 copy.41
  21.2 0.4 maximum_convert_fusion
  21.6 1.3 multiply_convert_fusion.5
  22.9 0.1 fusion.35
  23.0 0.1 maximum_select_fusion.1
  23.1 4.6 %collective-permute-start.1 = (bf16[512,256]{1,0:T(8,128)(2,1)S(1)}, bf16[512,256]{1,0:T(8,128)(2,1)S(1)}, u32[]{:S(2)}, u32[]{:S(2)}) collective-permute-start(bf16[512,256]{1,0:T(8,128)(2,1)S(1)} %maximum_select_fusion.1), channel_id=1, source_target_pairs={{0,2},{1,3},{2,0},{3,1},{4,6},{5,7},{6,4},{7,5},{8,10},{9,11},{10,... | collective-permute-start | bytes 786440 | tf_op jit(solution)/shard_map/ppermute | solution.py:13
  27.7 0.1 add_bitcast_fusion.1
  27.8 1.0 copy.44
  28.8 0.1 maximum_select_fusion.2
  28.9 5.3 %collective-permute-done.1 = bf16[512,256]{1,0:T(8,128)(2,1)S(1)} collective-permute-done((bf16[512,256]{1,0:T(8,128)(2,1)S(1)}, bf16[512,256]{1,0:T(8,128)(2,1)S(1)}, u32[]{:S(2)}, u32[]{:S(2)}) %collective-permute-start.1) | collective-permute-done | bytes 262176 | tf_op jit(solution)/shard_map/ppermute | solution.py:13
  34.2 0.1 maximum_select_fusion
  34.3 0.3 fusion.29
  34.6 1.4 fusion.7
  36.1 0.8 fusion.9
  36.9 0.8 copy.43
  37.7 0.1 copy.50
  37.8 0.4 multiply_reduce_fusion
  38.2 2.4 collective-permute-start.2
  40.6 3.0 collective-permute-done.2
  43.6 4.6 %collective-permute-start.3 = (f32[1,512]{1,0:T(1,128)S(1)}, f32[1,512]{1,0:T(1,128)S(1)}, u32[]{:S(2)}, u32[]{:S(2)}) collective-permute-start(f32[1,512]{1,0:T(1,128)S(1)} %add.115), channel_id=1, source_target_pairs={{0,2},{1,3},{2,0},{3,1},{4,6},{5,7},{6,4},{7,5},{8,10},{9,11},{10,... | collective-permute-start | bytes 6152 | tf_op jit(solution)/shard_map/ppermute | solution.py:13
  48.3 2.3 collective-permute-done.3
  50.6 82.7 %all-gather.2.cloned.1.call-done = bf16[512,4096]{1,0:T(8,128)(2,1)} async-done(((bf16[512,256]{1,0:T(8,128)(2,1)}), bf16[512,4096]{1,0:T(8,128)(2,1)}) %all-gather.2.cloned.1.call-update) | async-done | bytes 4194320 | tf_op jit(solution)/shard_map/all_gather | solution.py:123
  133.3 6.8 %convolution_convert_fusion = bf16[512,4096]{1,0:T(8,128)(2,1)} fusion(bf16[512,4096]{1,0:T(8,128)(2,1)} %all-gather.2.cloned.1.call-done, f32[512]{0:T(512)S(1)} %copy-done.7, f32[512]{0:T(512)S(1)} %bitcast.86, f32[512,512]{0,1:T(8,128)S(1)} %bitcast.66, bf16[512,512]{0,1:T(8,128)(2,1)} %copy.44), kind=kOutput, calls=%fused_computation | convolution fusion | flops 2151940096 | bytes 9965568 | tf_op jit(solution)/shard_map/dot_general | solution.py:121
  140.2 6.5 %copy.48 = bf16[512,4096]{0,1:T(8,128)(2,1)} copy(bf16[512,4096]{1,0:T(8,128)(2,1)} %convolution_convert_fusion) | data formatting | bytes 8388608
  146.6 0.0 reduce-scatter.4.cloned.1.call-update
  146.7 0.2 slice_reduce_fusion.1
  146.8 0.1 exponential_multiply_fusion
  146.9 1.7 convolution_add_fusion
  148.6 241.6 %reduce-scatter.4.cloned.1.call-done = bf16[128,512]{1,0:T(8,128)(2,1)} async-done(((bf16[4096,512]{1,0:T(8,128)(2,1)}), bf16[128,512]{1,0:T(8,128)(2,1)}) %reduce-scatter.4.cloned.1.call-update) | async-done | bytes 131088
  390.2 1.7 copy.49
  (24 shorter events, 0.2 us)
Async XLA Ops:
  7.2 13.8 %copy-start.2 = (bf16[512,512]{1,0:T(8,128)(2,1)S(1)}, bf16[512,512]{1,0:T(8,128)(2,1)}, u32[]{:S(2)}) copy-start(bf16[512,512]{1,0:T(8,128)(2,1)} %param.17) | copy-start | bytes 1572868
  7.2 14.4 %copy-start.4 = (f32[4,512]{1,0:T(4,128)S(1)}, f32[4,512]{1,0:T(4,128)}, u32[]{:S(2)}) copy-start(f32[4,512]{1,0:T(4,128)} %param.23) | copy-start | bytes 24580
  7.2 14.4 %copy-start.5 = (f32[512]{0:T(512)S(1)}, f32[512]{0:T(512)}, u32[]{:S(2)}) copy-start(f32[512]{0:T(512)} %param.24) | copy-start | bytes 6148
  7.2 126.1 %all-gather.2.cloned.1.call-start = ((), (), s32[]{:S(2)}) async-start(), calls=%async_computation.1 | async-start | bytes 4456448 | tf_op jit(solution)/shard_map/all_gather | solution.py:123
  10.4 379.8 %reduce-scatter.4.cloned.1.call-start = ((), (), s32[]{:S(2)}) async-start(), calls=%async_computation.2 | async-start | bytes 4325376
  13.8 9.2 %collective-permute-start = (bf16[512,128]{1,0:T(8,128)(2,1)S(1)}, bf16[512,128]{1,0:T(8,128)(2,1)S(1)}, u32[]{:S(2)}, u32[]{:S(2)}) collective-permute-start(bf16[512,128]{1,0:T(8,128)(2,1)S(1)} %bitcast.69), channel_id=1, source_target_pairs={{0,1},{1,0},{2,3},{3,2},{4,5},{5,4},{6,7},{7,6},{8,9},{9,8},{10,11... | collective-permute-start | bytes 393224 | tf_op jit(solution)/shard_map/ppermute | solution.py:13
  21.0 6.8 %copy-start.3 = (bf16[512,512]{1,0:T(8,128)(2,1)S(1)}, bf16[512,512]{1,0:T(8,128)(2,1)}, u32[]{:S(2)}) copy-start(bf16[512,512]{1,0:T(8,128)(2,1)} %param.18) | copy-start | bytes 1572868
  23.1 11.2 %collective-permute-start.1 = (bf16[512,256]{1,0:T(8,128)(2,1)S(1)}, bf16[512,256]{1,0:T(8,128)(2,1)S(1)}, u32[]{:S(2)}, u32[]{:S(2)}) collective-permute-start(bf16[512,256]{1,0:T(8,128)(2,1)S(1)} %maximum_select_fusion.1), channel_id=1, source_target_pairs={{0,2},{1,3},{2,0},{3,1},{4,6},{5,7},{6,4},{7,5},{8,10},{9,11},{10,... | collective-permute-start | bytes 786440 | tf_op jit(solution)/shard_map/ppermute | solution.py:13
  34.6 1.4 copy-start
  34.6 1.4 copy-start.6
  36.0 1.8 copy-start.1
  36.1 97.3 %copy-start.7 = (f32[512]{0:T(512)S(1)}, f32[512]{0:T(512)}, u32[]{:S(2)}) copy-start(f32[512]{0:T(512)} %param.31) | copy-start | bytes 6148
  38.2 5.5 %collective-permute-start.2 = (f32[1,512]{1,0:T(1,128)S(1)}, f32[1,512]{1,0:T(1,128)S(1)}, u32[]{:S(2)}, u32[]{:S(2)}) collective-permute-start(f32[1,512]{1,0:T(1,128)S(1)} %bitcast.80), channel_id=1, source_target_pairs={{0,1},{1,0},{2,3},{3,2},{4,5},{5,4},{6,7},{7,6},{8,9},{9,8},{10,11... | collective-permute-start | bytes 6152 | tf_op jit(solution)/shard_map/ppermute | solution.py:13
  43.6 7.0 %collective-permute-start.3 = (f32[1,512]{1,0:T(1,128)S(1)}, f32[1,512]{1,0:T(1,128)S(1)}, u32[]{:S(2)}, u32[]{:S(2)}) collective-permute-start(f32[1,512]{1,0:T(1,128)S(1)} %add.115), channel_id=1, source_target_pairs={{0,2},{1,3},{2,0},{3,1},{4,6},{5,7},{6,4},{7,5},{8,10},{9,11},{10,... | collective-permute-start | bytes 6152 | tf_op jit(solution)/shard_map/ppermute | solution.py:13
Sparse Core Ops, SparseCore 0:
  11.2 122.0 all-gather.1
  146.8 243.3 reduce-scatter.3
where the time goes:
time: 399 us
  waiting for transfers between devices  335 us (84%)
  starting transfers between devices  15.2 us (4%)
  local copies, waits for them, and re-layouts  14.5 us (4%)
  between operations  14.3 us (4%)
  matrix products  11 us (3%)
  other arithmetic  8.77 us (2%)
    unnamed x3, waiting for transfers between devices  242 us
    all_gather x1, waiting for transfers between devices, per_device(): lax.all_gather(weight_local, 'fsdp', axis=1, tiled=True)  82.7 us
    ppermute x4, starting transfers between devices, partner_2(): lax.ppermute(shard, axis, [(i, i ^ 1 << stride) for i in range(lax.axis_s...  15.1 us
    unnamed x23, local copies, waits for them, and re-layouts  11.6 us
    ppermute x4, waiting for transfers between devices, partner_2(): lax.ppermute(shard, axis, [(i, i ^ 1 << stride) for i in range(lax.axis_s...  10.7 us
  transfers between devices with their start and end apart: 6, of which 5 were waited for; matrix products, arithmetic and copies ran while one was open for 4% of the time, Pallas kernels for 0%

commit v1 on v0

v1 whole, which is shorter than its diff:
```python
import functools

import jax
import jax.numpy as jnp
from jax import lax
from jax.experimental import pallas as pl
from jax.experimental.pallas import tpu as pltpu
from jax.sharding import PartitionSpec as P

EPS = 1e-05
MESH = pl.DeviceIdType.MESH
F32 = jnp.float32
BF16 = jnp.bfloat16
NEG = -1e30
HIGHEST = lax.Precision.HIGHEST


def silu(v):
    return v / (1.0 + jnp.exp(-v))


def dot_nt(a, b):
    return lax.dot_general(a, b, (((1,), (1,)), ((), ())), preferred_element_type=F32)


def dot_tn(a, b):
    return lax.dot_general(a, b, (((0,), (0,)), ((), ())), preferred_element_type=F32)


def dot_nn(a, b):
    return jnp.dot(a, b, preferred_element_type=F32)


def kernel(
    xs, gate, bc, dt, x_tail, bc_tail, cxw, cxb, cbw, cbb, dt_bias, a_log, skip_d, state, gain,
    values, scales,
    out, new_state,
    wsrc, wfull, bcall, gall, xact, conv_x, conv_b, ldc, stc, ldr, stp, score, part, sbuf, rbuf,
    a2a_send, a2a_recv, y_send, z_send, w_recv, sib_send, sib_recv, bc_send, bc_recv,
    g_send, g_recv, s_send, s_recv,
):
    f = lax.axis_index("fsdp")
    ch = lax.axis_index("chan")
    zh, y, c = lax.div(f, 8), lax.rem(lax.div(f, 2), 4), lax.rem(f, 2)
    zl, x = lax.div(ch, 4), lax.rem(ch, 4)
    x_owner = lax.div(x, 2)
    d_me = zh * 4 + y
    d_far = (1 - zh) * 4 + y

    def at(zh=zh, y=y, c=c, zl=zl, x=x):
        return ((zh * 4 + y) * 2 + c, zl * 4 + x)

    def xn(j, core=c):
        return at(x=lax.rem(x + j, 4), c=core)

    def yn(j):
        return at(y=lax.rem(y + j, 4))

    def zn(step):
        z = lax.rem(zh * 8 + zl + step, 16)
        return at(zh=lax.div(z, 8), zl=lax.rem(z, 8))

    sibling = at(c=1 - c)
    opposite = at(zh=1 - zh)

    def rcopy(src, dst, send, recv, device):
        return pltpu.make_async_remote_copy(
            src_ref=src, dst_ref=dst, send_sem=send, recv_sem=recv, device_id=device,
            device_id_type=MESH,
        )

    bar = pltpu.get_barrier_semaphore()
    others = [xn(j, core) for j in (1, 2, 3) for core in (c, 1 - c)]
    others += [yn(j) for j in (1, 2, 3)] + [zn(1), zn(15), opposite, sibling]
    for device in others:
        pl.semaphore_signal(bar, inc=1, device_id=device, device_id_type=MESH)
    gain_rows = jnp.transpose(jnp.broadcast_to(gain[...], (128, 512)))
    for k in range(4):
        for b in range(2):
            tile = values[k * 128:(k + 1) * 128, b * 128:(b + 1) * 128].astype(F32)
            tile = tile * scales[k, b] * gain_rows[k * 128:(k + 1) * 128]
            wsrc[b, k] = tile.astype(BF16)
    pl.semaphore_wait(bar, len(others))

    def a2a(b, q):
        return rcopy(
            wsrc.at[b, pl.ds(2 * q, 2)], wfull.at[d_me, pl.ds(2 * q, 2), x],
            a2a_send.at[b, q], a2a_recv.at[x], at(x=2 * c + b, c=q),
        )

    def a2a_local(b, q):
        return jnp.logical_and(x == 2 * c + b, c == q)

    for b in range(2):
        for q in range(2):
            @pl.when(jnp.logical_not(a2a_local(b, q)))
            def _():
                a2a(b, q).start()

            @pl.when(a2a_local(b, q))
            def _():
                wfull[d_me, 2 * q, x] = wsrc[b, 2 * q]
                wfull[d_me, 2 * q + 1, x] = wsrc[b, 2 * q + 1]

    def conv(scratch, rows, tail, w, b, lanes):
        scratch[5:8, lanes] = tail.astype(F32)
        scratch[8:264, lanes] = rows.astype(F32)
        total = b[:, lanes]
        for k in range(4):
            total = total + w[k:k + 1, lanes] * scratch[5 + k:261 + k, lanes]
        return silu(total).astype(BF16)

    def bc_copy(r, j):
        return rcopy(
            bcall.at[x, r], bcall.at[x, r], bc_send.at[r, j - 1], bc_recv.at[x, r], xn(j)
        )

    for r in range(2):
        bcall[x, r] = conv(conv_b, bc[r], bc_tail[r], cbw, cbb, slice(0, 128))
        for j in (1, 3, 2):
            bc_copy(r, j).start()

    row = lax.broadcasted_iota(jnp.int32, (256, 256), 0)
    col = lax.broadcasted_iota(jnp.int32, (256, 256), 1)
    tril = (row >= col).astype(F32)
    rate = jnp.exp(a_log[...])

    def prepare(r):
        v = dt[r] + dt_bias[...]
        step = jnp.maximum(v, 0.0) + jnp.log1p(jnp.exp(-jnp.abs(v)))
        ldc[r] = jnp.zeros((256, 128), F32)
        stc[r] = jnp.zeros((256, 128), F32)
        ldc[r, :, 0:8] = jnp.dot(
            tril, -rate * step, precision=HIGHEST, preferred_element_type=F32
        )
        stc[r, :, 0:8] = step
        ldr[r] = jnp.transpose(ldc[r])[0:8]
        stp[r] = jnp.transpose(stc[r])[0:8]
        for p in range(4):
            lanes = slice(p * 128, (p + 1) * 128)
            xact[r, p] = conv(conv_x, xs[r, :, lanes], x_tail[r, :, lanes], cxw, cxb, lanes)

    lane = lax.broadcasted_iota(jnp.int32, (1, 128), 1)
    low = lane < 64
    r128 = lax.broadcasted_iota(jnp.int32, (128, 128), 0)
    c128 = lax.broadcasted_iota(jnp.int32, (128, 128), 1)
    upper = jnp.where(r128 >= c128, 0.0, NEG)

    def pick(table, r, p, rows=slice(None)):
        return jnp.where(
            low, table[r, rows, 2 * p:2 * p + 1], table[r, rows, 2 * p + 1:2 * p + 2]
        )

    def b_rows(r):
        return jnp.concatenate([bcall[0, r], bcall[1, r]], axis=1)

    def ssd(r):
        c_rows = jnp.concatenate([bcall[2, r], bcall[3, r]], axis=1)
        score[...] = dot_nt(c_rows, b_rows(r))
        for p in range(4):
            lanes = slice(p * 128, (p + 1) * 128)
            xp = xact[r, p]
            masked = [jnp.where(low, xp, 0).astype(BF16), jnp.where(low, 0, xp).astype(BF16)]
            top, bottom = [], []
            for e in range(2):
                h = 2 * p + e

                def mix(i, j):
                    ri, rj = slice(i * 128, i * 128 + 128), slice(j * 128, j * 128 + 128)
                    spread = ldc[r, ri, h:h + 1] - ldr[r, h:h + 1, rj]
                    if i == j:
                        spread = spread + upper
                        spread = jnp.minimum(spread, 0.0)
                    return (score[ri, rj] * jnp.exp(spread) * stp[r, h:h + 1, rj]).astype(BF16)

                top.append(mix(0, 0))
                bottom += [mix(1, 0), mix(1, 1)]
            y_top = dot_nn(
                jnp.concatenate(top, axis=1),
                jnp.concatenate([masked[0][:128], masked[1][:128]], axis=0),
            )
            y_bottom = dot_nn(
                jnp.concatenate(bottom, axis=1), jnp.concatenate(masked, axis=0)
            )
            held = state[r, 2 * p:2 * p + 2].reshape(128, 256).astype(BF16)
            from_state = dot_nt(c_rows, held)
            skip = jnp.where(low, skip_d[0, 2 * p], skip_d[0, 2 * p + 1])
            rows = jnp.concatenate([y_top, y_bottom], axis=0)
            rows = rows + from_state * jnp.exp(pick(ldc, r, p)) + skip * xp.astype(F32)
            gall[r, x, p] = (rows * silu(gate[r, :, lanes].astype(F32))).astype(BF16)

    def carry(r):
        for p in range(4):
            last = pick(ldc, r, p, slice(255, 256))
            weight = jnp.exp(last - pick(ldc, r, p)) * pick(stc, r, p)
            xw = (xact[r, p].astype(F32) * weight).astype(BF16)
            update = dot_tn(xw, b_rows(r))
            for e in range(2):
                h = 2 * p + e
                decay = jnp.exp(ldc[r, 255:256, h:h + 1])
                new_state[r, h] = decay * state[r, h] + update[e * 64:(e + 1) * 64]

    def y_copy(half, d, s, j):
        piece = wfull.at[d, 2 * c + s]
        return rcopy(piece, piece, y_send.at[half, s, j - 1], w_recv.at[d, s], yn(j))

    def z_copy(s):
        piece = wfull.at[d_me, 2 * c + s]
        return rcopy(piece, piece, z_send.at[s], w_recv.at[d_me, s], opposite)

    def sib_copy(d, s):
        piece = wfull.at[d, 2 * c + s]
        return rcopy(piece, piece, sib_send.at[d, s], sib_recv.at[d, s], sibling)

    def w_wait(d, s):
        piece = wfull.at[d, 2 * c + s]
        rcopy(piece, piece, z_send.at[s], w_recv.at[d, s], opposite).wait_recv()

    def sib_wait(d, s):
        piece = wfull.at[d, 2 * (1 - c) + s]
        rcopy(piece, piece, sib_send.at[d, s], sib_recv.at[d, s], sibling).wait_recv()

    def spread_own():
        for j in range(4):
            @pl.when(jnp.logical_not(jnp.logical_and(x == j, c == x_owner)))
            def _():
                rcopy(
                    wsrc.at[0, pl.ds(0, 2)], wfull.at[d_me, pl.ds(2 * c, 2), j],
                    a2a_send.at[0, 0], a2a_recv.at[j], sibling,
                ).wait_recv()

        for s in range(2):
            z_copy(s).start()
        for s in range(2):
            for j in (1, 3, 2):
                y_copy(0, d_me, s, j).start()
            sib_copy(d_me, s).start()

    def spread_far(s):
        w_wait(d_far, s)
        for j in (1, 3, 2):
            y_copy(1, d_far, s, j).start()
        sib_copy(d_far, s).start()

    def hand_over(half, s):
        for j in (1, 3, 2):
            d = half * 4 + lax.rem(y + j, 4)
            w_wait(d, s)
            sib_copy(d, s).start()

    def sib_all(half):
        for i in range(4):
            for s in range(2):
                sib_wait(half * 4 + i, s)

    def g_copy(r, j):
        return rcopy(gall.at[r, x], gall.at[r, x], g_send.at[r, j - 1], g_recv.at[r, x], xn(j))

    def g_start(r):
        for j in (1, 3, 2):
            g_copy(r, j).start()

    def g_wait(r):
        for j in (1, 3, 2):
            source = lax.rem(x + j, 4)
            slot = gall.at[r, source]
            rcopy(slot, slot, g_send.at[r, j - 1], g_recv.at[r, source], xn(j)).wait_recv()

    def bc_wait(r):
        for j in (1, 3, 2):
            source = lax.rem(x + j, 4)
            slot = bcall.at[source, r]
            rcopy(slot, slot, bc_send.at[r, j - 1], bc_recv.at[source, r], xn(j)).wait_recv()

    def row_factor(r):
        total = jnp.zeros((256, 128), F32)
        for k in range(4):
            for j in range(4):
                block = gall[r, j, k].astype(F32)
                total = total + block * block
        return lax.rsqrt(jnp.sum(total, axis=1, keepdims=True) / 2048.0 + EPS)

    def project(r, half):
        factor = row_factor(r)
        rows = jnp.concatenate([gall[r, j, k] for k in range(4) for j in range(4)], axis=1)
        for i in range(2):
            d = half * 4 + 2 * i
            both = jnp.concatenate(
                [wfull[d].reshape(2048, 128), wfull[d + 1].reshape(2048, 128)], axis=1
            )
            product = dot_nn(rows, both) * factor
            part[r, d] = product[:, :128]
            part[r, d + 1] = product[:, 128:]

    def s_copy(r, d, way):
        target = at(zl=zl + 1 - 2 * way)
        return rcopy(
            sbuf.at[r, d], rbuf.at[way, r, d], s_send.at[r, d], s_recv.at[way, r, d], target
        )

    def s_wait(r, d, way):
        slot = rbuf.at[way, r, d]
        rcopy(slot, slot, s_send.at[r, d], s_recv.at[way, r, d], sibling).wait_recv()

    def order(half, i):
        seat = zl + half * (7 - 2 * zl)
        near = jnp.maximum(3 - seat, 0)
        d = jnp.where(i < near, 3 - i, i - near)
        inside = seat < 4
        return d + half * (7 - 2 * d), near, inside

    def relay(r, d):
        way = (d < zl).astype(jnp.int32)
        fed = (zl + way * (7 - 2 * zl)) > 0

        @pl.when(fed)
        def _():
            s_wait(r, d, way)
            sbuf[r, d] = (part[r, d] + rbuf[way, r, d].astype(F32)).astype(BF16)

        @pl.when(jnp.logical_not(fed))
        def _():
            sbuf[r, d] = part[r, d].astype(BF16)

        s_copy(r, d, way).start()

    def relay_near(r, half):
        def body(i, carry_):
            d, near, inside = order(half, i)

            @pl.when(jnp.logical_or(jnp.logical_not(inside), i < near))
            def _():
                relay(r, d)

            return carry_

        lax.fori_loop(0, 4, body, 0)

    def relay_far(r, half):
        def body(i, carry_):
            d, near, inside = order(half, i)

            @pl.when(jnp.logical_and(inside, i >= near))
            def _():
                relay(r, d)

            return carry_

        lax.fori_loop(0, 3, body, 0)

    def finish(r):
        @pl.when(zl > 0)
        def _():
            s_wait(r, zl, 0)
            part[r, zl] = part[r, zl] + rbuf[0, r, zl].astype(F32)

        @pl.when(zl < 7)
        def _():
            s_wait(r, zl, 1)
            part[r, zl] = part[r, zl] + rbuf[1, r, zl].astype(F32)

        out[r] = part[r, zl].astype(BF16)

    prepare(0)
    spread_own()
    prepare(1)
    bc_wait(0)
    ssd(0)
    g_start(0)
    bc_wait(1)
    ssd(1)
    g_start(1)
    for s in range(2):
        hand_over(zh, s)
    carry(0)
    carry(1)
    spread_far(0)
    sib_all(zh)
    g_wait(0)
    project(0, zh)
    relay_near(0, zh)
    g_wait(1)
    project(1, zh)
    relay_near(1, zh)
    hand_over(1 - zh, 0)
    spread_far(1)
    relay_far(0, zh)
    relay_far(1, zh)
    hand_over(1 - zh, 1)
    sib_all(1 - zh)
    project(0, 1 - zh)
    relay_near(0, 1 - zh)
    project(1, 1 - zh)
    relay_near(1, 1 - zh)
    relay_far(0, 1 - zh)
    relay_far(1, 1 - zh)
    finish(0)
    finish(1)

    for b in range(2):
        for q in range(2):
            @pl.when(jnp.logical_not(a2a_local(b, q)))
            def _():
                a2a(b, q).wait_send()
    for s in range(2):
        z_copy(s).wait_send()
        for j in (1, 2, 3):
            y_copy(0, d_me, s, j).wait_send()
            y_copy(1, d_far, s, j).wait_send()
        for d in range(8):
            sib_copy(d, s).wait_send()
    for r in range(2):
        for j in (1, 2, 3):
            bc_copy(r, j).wait_send()
            g_copy(r, j).wait_send()
        for d in range(8):
            @pl.when(d != zl)
            def _():
                s_copy(r, d, (d < zl).astype(jnp.int32)).wait_send()


def per_device(
    xs_in, gate_in, bc_in, dt_raw, x_tail, bc_tail, conv_x_w, conv_x_b, conv_bc_w, conv_bc_b,
    dt_bias, a_log, skip_d, state_in, norm_gain, out_values, out_scales,
):
    vmem = pl.BlockSpec(memory_space=pltpu.VMEM)
    smem = pl.BlockSpec(memory_space=pltpu.SMEM)
    dma = pltpu.SemaphoreType.DMA
    out, new_state = pl.pallas_call(
        kernel,
        name="mixer",
        out_shape=(
            jax.ShapeDtypeStruct((2, 256, 128), BF16),
            jax.ShapeDtypeStruct(state_in.shape, F32),
        ),
        in_specs=[vmem] * 12 + [smem] + [vmem] * 3 + [smem],
        out_specs=(vmem, vmem),
        scratch_shapes=[
            pltpu.VMEM((2, 4, 128, 128), BF16),
            pltpu.VMEM((8, 4, 4, 128, 128), BF16),
            pltpu.VMEM((4, 2, 256, 128), BF16),
            pltpu.VMEM((2, 4, 4, 256, 128), BF16),
            pltpu.VMEM((2, 4, 256, 128), BF16),
            pltpu.VMEM((264, 512), F32),
            pltpu.VMEM((264, 128), F32),
            pltpu.VMEM((2, 256, 128), F32),
            pltpu.VMEM((2, 256, 128), F32),
            pltpu.VMEM((2, 8, 256), F32),
            pltpu.VMEM((2, 8, 256), F32),
            pltpu.VMEM((256, 256), F32),
            pltpu.VMEM((2, 8, 256, 128), F32),
            pltpu.VMEM((2, 8, 256, 128), BF16),
            pltpu.VMEM((2, 2, 8, 256, 128), BF16),
            dma((2, 2)),
            dma((4,)),
            dma((2, 2, 3)),
            dma((2,)),
            dma((8, 2)),
            dma((8, 2)),
            dma((8, 2)),
            dma((2, 3)),
            dma((4, 2)),
            dma((2, 3)),
            dma((2, 4)),
            dma((2, 8)),
            dma((2, 2, 8)),
        ],
        compiler_params=pltpu.CompilerParams(
            collective_id=0, has_side_effects=True, vmem_limit_bytes=44 * 1024 * 1024
        ),
    )(
        xs_in.reshape(2, 256, 512), gate_in.reshape(2, 256, 512), bc_in.reshape(2, 256, 128),
        dt_raw.reshape(2, 256, 8), x_tail, bc_tail, conv_x_w, conv_x_b.reshape(1, 512),
        conv_bc_w, conv_bc_b.reshape(1, 128), dt_bias.reshape(1, 8), a_log.reshape(1, 8),
        skip_d.reshape(1, 8), state_in, norm_gain.reshape(1, 512), out_values, out_scales,
    )
    return out.reshape(512, 128), new_state


def solution(mesh):
    placed = (
        P("fsdp", "chan"),
        P("fsdp", "chan"),
        P("fsdp", "chan"),
        P("fsdp", "chan"),
        P("fsdp", None, "chan"),
        P("fsdp", None, "chan"),
        P(None, "chan"),
        P("chan"),
        P(None, "chan"),
        P("chan"),
        P("chan"),
        P("chan"),
        P("chan"),
        P("fsdp", "chan", None, None),
        P("chan"),
        P("chan", "fsdp"),
        P("chan", "fsdp"),
    )
    return jax.shard_map(
        per_device,
        mesh=mesh,
        in_specs=placed,
        out_specs=(P("fsdp", "chan"), P("fsdp", "chan", None, None)),
        check_vma=False,
    )
```

time: 399 us -> 105 us (0.26)
  the two profiles are of different devices: /device:TPU:8 before, /device:TPU:224 now
where the time goes in v1:
time: 105 us
  Pallas kernels  94.3 us (90%)
  local copies, waits for them, and re-layouts  9.54 us (9%)
    pallas_call x1, Pallas kernels, per_device(): pl.pallas_call(kernel, name='mixer', out_shape=(jax.ShapeDtypeStruct((2,...  94.3 us
    unnamed x32, local copies, waits for them, and re-layouts  9.54 us

profile of v1, /device:TPU:224, one launch (start us, length us, event | category | flops | bytes accessed | tf_op | source)
XLA Modules:
  0.0 104.6 jit_solution(7911117382766010497)
XLA Ops:
  0.6 0.0 copy-start.3
  0.6 0.7 copy.21.bc_tail
  1.4 0.8 copy.22.scales
  2.1 0.7 copy.20.x_tail
  2.8 0.0 copy-start.5
  2.8 0.0 copy-start.6
  2.8 0.0 copy-start.7
  2.8 0.0 copy-start.8
  2.9 0.0 copy-start.12
  2.9 0.9 copy.19
  3.8 0.0 copy-start.9
  3.8 0.0 copy-start.10
  3.8 0.0 copy-start.11
  3.8 0.0 copy-done.3
  3.8 0.0 copy-done.5
  3.8 0.0 copy-done.6
  3.8 0.0 copy-done.7
  3.8 0.0 copy-done.8
  3.8 0.0 copy-done.12
  3.8 0.6 copy-done.9
  4.4 0.0 copy-done.10
  4.4 0.0 copy-done.11
  4.4 0.0 copy-start
  4.4 1.2 %copy-done = f32[2,8,64,256]{3,2,1,0:T(8,128)S(1)} copy-done((f32[2,8,64,256]{3,2,1,0:T(8,128)S(1)}, f32[2,8,64,256]{3,2,1,0:T(8,128)}, u32[]{:S(2)}) %copy-start) | copy-done | bytes 1048600
  5.7 0.0 copy-start.1
  5.7 1.0 copy-done.1
  6.7 0.0 copy-start.2
  6.7 1.0 copy-done.2
  7.8 0.0 copy-start.4
  7.8 0.9 copy-done.4
  8.7 94.3 %mixer.1 = (bf16[2,256,128]{2,1,0:T(8,128)(2,1)S(1)}, f32[2,8,64,256]{3,2,1,0:T(8,128)S(1)}) custom-call(bf16[2,256,512]{2,1,0:T(8,128)(2,1)S(1)} %bitcast.12, bf16[2,256,512]{2,1,0:T(8,128)(2,1)S(1)} %bitcast.13, bf16[2,256,128]{2,1,0:T(8,128)(2,1)S(1)} %bitcast.14, f32[2,256,8]{2,1,0:T(8,128)S(1)} %bitcast.11, bf16[2,3,512]{2,1,0:T(4,128)(2,1)S(1)} %copy.20.x_tail, ...), custom_call_target="tpu_custom_call" | custom-call | tf_op jit(solution)/shard_map/mixer/pallas_call | solution.py:429
  102.9 0.7 copy.25
  103.6 1.0 copy.26
Async XLA Ops:
  0.6 3.2 %copy-start.3 = (bf16[512,256]{1,0:T(8,128)(2,1)S(1)}, bf16[512,256]{1,0:T(8,128)(2,1)}, u32[]{:S(2)}) copy-start(bf16[512,256]{1,0:T(8,128)(2,1)} %values.1) | copy-start | bytes 786436
  2.8 1.0 copy-start.5
  2.8 1.0 copy-start.6
  2.8 1.0 copy-start.7
  2.8 1.0 copy-start.8
  2.9 1.0 copy-start.12
  3.8 0.7 copy-start.9
  3.8 0.7 copy-start.10
  3.8 0.7 copy-start.11
  4.4 1.2 %copy-start = (f32[2,8,64,256]{3,2,1,0:T(8,128)S(1)}, f32[2,8,64,256]{3,2,1,0:T(8,128)}, u32[]{:S(2)}) copy-start(f32[2,8,64,256]{3,2,1,0:T(8,128)} %state.1) | copy-start | bytes 3145732
  5.7 1.0 copy-start.1
  6.7 1.0 copy-start.2
  7.8 0.9 copy-start.4

commit v2 on v1

--- a/solution.py
+++ b/solution.py
@@ -31,14 +31,17 @@
     return jnp.dot(a, b, preferred_element_type=F32)
 
 
-def kernel(
-    xs, gate, bc, dt, x_tail, bc_tail, cxw, cxb, cbw, cbb, dt_bias, a_log, skip_d, state, gain,
-    values, scales,
-    out, new_state,
-    wsrc, wfull, bcall, gall, xact, conv_x, conv_b, ldc, stc, ldr, stp, score, part, sbuf, rbuf,
-    a2a_send, a2a_recv, y_send, z_send, w_recv, sib_send, sib_recv, bc_send, bc_recv,
-    g_send, g_recv, s_send, s_recv,
-):
+def kernel(*refs):
+    hbm, (out, state_out), held, refs = refs[:17], refs[17:19], refs[19:36], refs[36:]
+    (
+        xs, gate, bc, dt, x_tail, bc_tail, cxw, cxb, cbw, cbb, dt_bias, a_log, skip_d, state, gain,
+        values, scales,
+    ) = held
+    (
+        wsrc, wfull, bcall, gall, xact, conv_x, conv_b, ldc, stc, ldr, stp, score, part, sbuf,
+        rbuf, new_state, in_sem, out_sem, a2a_send, a2a_recv, y_send, z_send, w_recv, sib_send, sib_recv, bc_send,
+        bc_recv, g_send, g_recv, s_send, s_recv,
+    ) = refs
     f = lax.axis_index("fsdp")
     ch = lax.axis_index("chan")
     zh, y, c = lax.div(f, 8), lax.rem(lax.div(f, 2), 4), lax.rem(f, 2)
@@ -70,17 +73,42 @@
         )
 
     bar = pltpu.get_barrier_semaphore()
+    half_line, seat_line = lax.div(zl, 4), lax.rem(zl, 4)
+    depth = seat_line + half_line * (3 - 2 * seat_line)
     others = [xn(j, core) for j in (1, 2, 3) for core in (c, 1 - c)]
     others += [yn(j) for j in (1, 2, 3)] + [zn(1), zn(15), opposite, sibling]
-    for device in others:
+    for device in others + [at(zl=4 - half_line)]:
         pl.semaphore_signal(bar, inc=1, device_id=device, device_id_type=MESH)
+
+    def fetch(i):
+        return pltpu.make_async_copy(hbm[i], held[i], in_sem.at[i])
+
+    for i in (15, 14, 16, 2, 5, 8, 9, 3, 10, 11, 0, 4, 6, 7, 13, 1, 12):
+        fetch(i).start()
+
+    for i in (15, 14, 16):
+        fetch(i).wait()
     gain_rows = jnp.transpose(jnp.broadcast_to(gain[...], (128, 512)))
     for k in range(4):
         for b in range(2):
             tile = values[k * 128:(k + 1) * 128, b * 128:(b + 1) * 128].astype(F32)
-            tile = tile * scales[k, b] * gain_rows[k * 128:(k + 1) * 128]
+            tile = tile * scales[b:b + 1, k:k + 1] * gain_rows[k * 128:(k + 1) * 128]
             wsrc[b, k] = tile.astype(BF16)
-    pl.semaphore_wait(bar, len(others))
+
+    def conv(scratch, rows, tails, r, w, b, lanes):
+        for k in range(3):
+            scratch[5 + k:6 + k, lanes] = tails[k].astype(F32)[r:r + 1, lanes]
+        scratch[8:264, lanes] = rows.astype(F32)
+        total = b[:, lanes]
+        for k in range(4):
+            total = total + w[k:k + 1, lanes] * scratch[5 + k:261 + k, lanes]
+        return silu(total).astype(BF16)
+
+    for i in (2, 5, 8, 9):
+        fetch(i).wait()
+    for r in range(2):
+        bcall[x, r] = conv(conv_b, bc[r], bc_tail, r, cbw, cbb, slice(0, 128))
+    pl.semaphore_wait(bar, len(others) + jnp.where(depth == 3, 4, 0))
 
     def a2a(b, q):
         return rcopy(
@@ -102,31 +130,27 @@
                 wfull[d_me, 2 * q, x] = wsrc[b, 2 * q]
                 wfull[d_me, 2 * q + 1, x] = wsrc[b, 2 * q + 1]
 
-    def conv(scratch, rows, tail, w, b, lanes):
-        scratch[5:8, lanes] = tail.astype(F32)
-        scratch[8:264, lanes] = rows.astype(F32)
-        total = b[:, lanes]
-        for k in range(4):
-            total = total + w[k:k + 1, lanes] * scratch[5 + k:261 + k, lanes]
-        return silu(total).astype(BF16)
-
     def bc_copy(r, j):
         return rcopy(
             bcall.at[x, r], bcall.at[x, r], bc_send.at[r, j - 1], bc_recv.at[x, r], xn(j)
         )
 
     for r in range(2):
-        bcall[x, r] = conv(conv_b, bc[r], bc_tail[r], cbw, cbb, slice(0, 128))
         for j in (1, 3, 2):
             bc_copy(r, j).start()
 
     row = lax.broadcasted_iota(jnp.int32, (256, 256), 0)
     col = lax.broadcasted_iota(jnp.int32, (256, 256), 1)
     tril = (row >= col).astype(F32)
+    for i in (3, 10, 11):
+        fetch(i).wait()
     rate = jnp.exp(a_log[...])
 
     def prepare(r):
-        v = dt[r] + dt_bias[...]
+        turned = jnp.concatenate(
+            [dt[:, r * 256:(r + 1) * 256], jnp.zeros((120, 256), F32)], axis=0
+        )
+        v = jnp.transpose(turned)[:, 0:8] + dt_bias[...]
         step = jnp.maximum(v, 0.0) + jnp.log1p(jnp.exp(-jnp.abs(v)))
         ldc[r] = jnp.zeros((256, 128), F32)
         stc[r] = jnp.zeros((256, 128), F32)
@@ -136,9 +160,12 @@
         stc[r, :, 0:8] = step
         ldr[r] = jnp.transpose(ldc[r])[0:8]
         stp[r] = jnp.transpose(stc[r])[0:8]
+        if r == 0:
+            for i in (0, 4, 6, 7):
+                fetch(i).wait()
         for p in range(4):
             lanes = slice(p * 128, (p + 1) * 128)
-            xact[r, p] = conv(conv_x, xs[r, :, lanes], x_tail[r, :, lanes], cxw, cxb, lanes)
+            xact[r, p] = conv(conv_x, xs[r, :, lanes], x_tail, r, cxw, cxb, lanes)
 
     lane = lax.broadcasted_iota(jnp.int32, (1, 128), 1)
     low = lane < 64
@@ -184,10 +211,15 @@
             )
             held = state[r, 2 * p:2 * p + 2].reshape(128, 256).astype(BF16)
             from_state = dot_nt(c_rows, held)
-            skip = jnp.where(low, skip_d[0, 2 * p], skip_d[0, 2 * p + 1])
+            skip = jnp.where(
+                low, skip_d[0:1, 2 * p:2 * p + 1], skip_d[0:1, 2 * p + 1:2 * p + 2]
+            )
             rows = jnp.concatenate([y_top, y_bottom], axis=0)
             rows = rows + from_state * jnp.exp(pick(ldc, r, p)) + skip * xp.astype(F32)
             gall[r, x, p] = (rows * silu(gate[r, :, lanes].astype(F32))).astype(BF16)
+
+    def state_copy(r):
+        return pltpu.make_async_copy(new_state.at[r], state_out.at[r], out_sem.at[r])
 
     def carry(r):
         for p in range(4):
@@ -199,6 +231,7 @@
                 h = 2 * p + e
                 decay = jnp.exp(ldc[r, 255:256, h:h + 1])
                 new_state[r, h] = decay * state[r, h] + update[e * 64:(e + 1) * 64]
+        state_copy(r).start()
 
     def y_copy(half, d, s, j):
         piece = wfull.at[d, 2 * c + s]
@@ -292,78 +325,73 @@
             part[r, d] = product[:, :128]
             part[r, d + 1] = product[:, 128:]
 
-    def s_copy(r, d, way):
-        target = at(zl=zl + 1 - 2 * way)
+    def s_copy(r, d, way, target):
         return rcopy(
-            sbuf.at[r, d], rbuf.at[way, r, d], s_send.at[r, d], s_recv.at[way, r, d], target
+            sbuf.at[r, d], rbuf.at[way, r, d], s_send.at[r, d], s_recv.at[way, r, d],
+            at(zl=target),
         )
 
     def s_wait(r, d, way):
         slot = rbuf.at[way, r, d]
         rcopy(slot, slot, s_send.at[r, d], s_recv.at[way, r, d], sibling).wait_recv()
 
-    def order(half, i):
-        seat = zl + half * (7 - 2 * zl)
-        near = jnp.maximum(3 - seat, 0)
-        d = jnp.where(i < near, 3 - i, i - near)
-        inside = seat < 4
-        return d + half * (7 - 2 * d), near, inside
-
-    def relay(r, d):
-        way = (d < zl).astype(jnp.int32)
-        fed = (zl + way * (7 - 2 * zl)) > 0
-
+    def relay(r, d, fed, came, way, target):
         @pl.when(fed)
         def _():
-            s_wait(r, d, way)
-            sbuf[r, d] = (part[r, d] + rbuf[way, r, d].astype(F32)).astype(BF16)
+            s_wait(r, d, came)
+            sbuf[r, d] = (part[r, d] + rbuf[came, r, d].astype(F32)).astype(BF16)
 
         @pl.when(jnp.logical_not(fed))
         def _():
             sbuf[r, d] = part[r, d].astype(BF16)
 
-        s_copy(r, d, way).start()
-
-    def relay_near(r, half):
-        def body(i, carry_):
-            d, near, inside = order(half, i)
-
-            @pl.when(jnp.logical_or(jnp.logical_not(inside), i < near))
-            def _():
-                relay(r, d)
-
-            return carry_
-
-        lax.fori_loop(0, 4, body, 0)
-
-    def relay_far(r, half):
-        def body(i, carry_):
-            d, near, inside = order(half, i)
-
-            @pl.when(jnp.logical_and(inside, i >= near))
-            def _():
-                relay(r, d)
-
-            return carry_
-
-        lax.fori_loop(0, 3, body, 0)
+        s_copy(r, d, way, target).start()
+
+    def relay_all(r, half):
+        @pl.when(half_line == half)
+        def _():
+            def body(i, carry_):
+                flip = lax.div(seat_line, 2)
+                near = 3 - (seat_line + flip * (3 - 2 * seat_line))
+                spot = jnp.where(i < near, 3 - i, i - near)
+                d = half * 4 + spot + flip * (3 - 2 * spot)
+                way = (d < zl).astype(jnp.int32)
+                fed = seat_line + way * (3 - 2 * seat_line) > 0
+                relay(r, d, fed, way, way, zl + 1 - 2 * way)
+                return carry_
+
+            lax.fori_loop(0, 3, body, 0)
+
+        @pl.when(half_line != half)
+        def _():
+            def body(i, carry_):
+                d = half * 4 + i + half * (3 - 2 * i)
+                last = depth == 3
+                target = jnp.where(last, d, zl + 1 - 2 * half_line)
+                relay(r, d, depth > 0, 0, jnp.where(last, 2, 0), target)
+                return carry_
+
+            lax.fori_loop(0, 4, body, 0)
 
     def finish(r):
-        @pl.when(zl > 0)
+        @pl.when(seat_line > 0)
         def _():
             s_wait(r, zl, 0)
             part[r, zl] = part[r, zl] + rbuf[0, r, zl].astype(F32)
 
-        @pl.when(zl < 7)
+        @pl.when(seat_line < 3)
         def _():
             s_wait(r, zl, 1)
             part[r, zl] = part[r, zl] + rbuf[1, r, zl].astype(F32)
 
-        out[r] = part[r, zl].astype(BF16)
+        s_wait(r, zl, 2)
+        out[r] = (part[r, zl] + rbuf[2, r, zl].astype(F32)).astype(BF16)
 
     prepare(0)
     spread_own()
     prepare(1)
+    for i in (13, 1, 12):
+        fetch(i).wait()
     bc_wait(0)
     ssd(0)
     g_start(0)
@@ -378,25 +406,23 @@
     sib_all(zh)
     g_wait(0)
     project(0, zh)
-    relay_near(0, zh)
+    relay_all(0, zh)
     g_wait(1)
     project(1, zh)
-    relay_near(1, zh)
+    relay_all(1, zh)
     hand_over(1 - zh, 0)
     spread_far(1)
-    relay_far(0, zh)
-    relay_far(1, zh)
     hand_over(1 - zh, 1)
     sib_all(1 - zh)
     project(0, 1 - zh)
-    relay_near(0, 1 - zh)
+    relay_all(0, 1 - zh)
     project(1, 1 - zh)
-    relay_near(1, 1 - zh)
-    relay_far(0, 1 - zh)
-    relay_far(1, 1 - zh)
+    relay_all(1, 1 - zh)
     finish(0)
     finish(1)
 
+    for r in range(2):
+        state_copy(r).wait()
     for b in range(2):
         for q in range(2):
             @pl.when(jnp.logical_not(a2a_local(b, q)))
@@ -416,7 +442,7 @@
         for d in range(8):
             @pl.when(d != zl)
             def _():
-                s_copy(r, d, (d < zl).astype(jnp.int32)).wait_send()
+                s_copy(r, d, 0, d).wait_send()
 
 
 def per_device(
@@ -424,8 +450,15 @@
     dt_bias, a_log, skip_d, state_in, norm_gain, out_values, out_scales,
 ):
     vmem = pl.BlockSpec(memory_space=pltpu.VMEM)
-    smem = pl.BlockSpec(memory_space=pltpu.SMEM)
+    stay = pl.BlockSpec(memory_space=pltpu.HBM)
     dma = pltpu.SemaphoreType.DMA
+    operands = (
+        xs_in.reshape(2, 256, 512), gate_in.reshape(2, 256, 512), bc_in.reshape(2, 256, 128),
+        dt_raw.T, x_tail.transpose(1, 0, 2), bc_tail.transpose(1, 0, 2), conv_x_w,
+        conv_x_b.reshape(1, 512), conv_bc_w, conv_bc_b.reshape(1, 128), dt_bias.reshape(1, 8),
+        a_log.reshape(1, 8), skip_d.reshape(1, 8), state_in, norm_gain.reshape(1, 512),
+        out_values, out_scales.T,
+    )
     out, new_state = pl.pallas_call(
         kernel,
         name="mixer",
@@ -433,9 +466,9 @@
             jax.ShapeDtypeStruct((2, 256, 128), BF16),
             jax.ShapeDtypeStruct(state_in.shape, F32),
         ),
-        in_specs=[vmem] * 12 + [smem] + [vmem] * 3 + [smem],
-        out_specs=(vmem, vmem),
-        scratch_shapes=[
+        in_specs=[stay] * 17,
+        out_specs=(vmem, stay),
+        scratch_shapes=[pltpu.VMEM(a.shape, a.dtype) for a in operands] + [
             pltpu.VMEM((2, 4, 128, 128), BF16),
             pltpu.VMEM((8, 4, 4, 128, 128), BF16),
             pltpu.VMEM((4, 2, 256, 128), BF16),
@@ -450,7 +483,10 @@
             pltpu.VMEM((256, 256), F32),
             pltpu.VMEM((2, 8, 256, 128), F32),
             pltpu.VMEM((2, 8, 256, 128), BF16),
-            pltpu.VMEM((2, 2, 8, 256, 128), BF16),
+            pltpu.VMEM((3, 2, 8, 256, 128), BF16),
+            pltpu.VMEM((2, 8, 64, 256), F32),
+            dma((17,)),
+            dma((2,)),
             dma((2, 2)),
             dma((4,)),
             dma((2, 2, 3)),
@@ -463,17 +499,12 @@
             dma((2, 3)),
             dma((2, 4)),
             dma((2, 8)),
-            dma((2, 2, 8)),
+            dma((3, 2, 8)),
         ],
         compiler_params=pltpu.CompilerParams(
-            collective_id=0, has_side_effects=True, vmem_limit_bytes=44 * 1024 * 1024
+            collective_id=0, has_side_effects=True, vmem_limit_bytes=60 * 1024 * 1024
         ),
-    )(
-        xs_in.reshape(2, 256, 512), gate_in.reshape(2, 256, 512), bc_in.reshape(2, 256, 128),
-        dt_raw.reshape(2, 256, 8), x_tail, bc_tail, conv_x_w, conv_x_b.reshape(1, 512),
-        conv_bc_w, conv_bc_b.reshape(1, 128), dt_bias.reshape(1, 8), a_log.reshape(1, 8),
-        skip_d.reshape(1, 8), state_in, norm_gain.reshape(1, 512), out_values, out_scales,
-    )
+    )(*operands)
     return out.reshape(512, 128), new_state
 
 

time: 105 us -> 95.3 us (0.908)
  the two profiles are of different devices: /device:TPU:224 before, /device:TPU:129 now
where the time goes in v2:
time: 95.3 us; the launch traced here: 95.1 us
  Pallas kernels  90.6 us (95%)
  local copies, waits for them, and re-layouts  3.86 us (4%)
    pallas_call x1, Pallas kernels, per_device(): pl.pallas_call(kernel, name='mixer', out_shape=(jax.ShapeDtypeStruct((2,...  90.6 us
    unnamed x2, local copies, waits for them, and re-layouts  3.86 us

profile of v2, /device:TPU:129, one launch (start us, length us, event | category | flops | bytes accessed | tf_op | source)
XLA Modules:
  0.0 95.1 jit_solution(14852483390726213729)
XLA Ops:
  0.6 90.6 %mixer.1 = (bf16[2,256,128]{2,1,0:T(8,128)(2,1)}, f32[2,8,64,256]{3,2,1,0:T(8,128)}) custom-call(bf16[2,256,512]{2,1,0:T(8,128)(2,1)} %bitcast.14, bf16[2,256,512]{2,1,0:T(8,128)(2,1)} %bitcast.15, bf16[2,256,128]{2,1,0:T(8,128)(2,1)} %bitcast.16, f32[8,512]{1,0:T(8,128)} %bitcast.18, bf16[3,2,512]{2,1,0:T(2,128)(2,1)} %bitcast.19, ...), custom_call_target="tpu_custom_call" | custom-call | tf_op jit(solution)/shard_map/mixer/pallas_call | solution.py:462
  91.3 1.6 %copy.21 = bf16[512,128]{1,0:T(8,128)(2,1)} copy(bf16[512,128]{1,0:T(8,128)(2,1)} %bitcast.17) | data formatting | bytes 262144
  92.8 2.3 %copy.22 = f32[2,8,64,256]{3,2,1,0:T(8,128)} copy(f32[2,8,64,256]{3,2,1,0:T(8,128)} %get-tuple-element.9) | data formatting | bytes 2097152

commit v3 on v2

--- a/solution.py
+++ b/solution.py
@@ -38,8 +38,9 @@
         values, scales,
     ) = held
     (
-        wsrc, wfull, bcall, gall, xact, conv_x, conv_b, ldc, stc, ldr, stp, score, part, sbuf,
-        rbuf, new_state, in_sem, out_sem, a2a_send, a2a_recv, y_send, z_send, w_recv, sib_send, sib_recv, bc_send,
+        wsrc, wfar, wfull, bcall, gall, xact, conv_x, conv_b, ldc, stc, ldr, stp, score, part, sbuf,
+        rbuf, new_state, in_sem, out_sem, a2a_send, a2a_recv, y_send, z_send,
+        z_recv, w_recv, sib_send, sib_recv, bc_send,
         bc_recv, g_send, g_recv, s_send, s_recv,
     ) = refs
     f = lax.axis_index("fsdp")
@@ -93,7 +94,7 @@
         for b in range(2):
             tile = values[k * 128:(k + 1) * 128, b * 128:(b + 1) * 128].astype(F32)
             tile = tile * scales[b:b + 1, k:k + 1] * gain_rows[k * 128:(k + 1) * 128]
-            wsrc[b, k] = tile.astype(BF16)
+            wsrc[k % 2, b, k // 2] = tile.astype(BF16)
 
     def conv(scratch, rows, tails, r, w, b, lanes):
         for k in range(3):
@@ -110,34 +111,54 @@
         bcall[x, r] = conv(conv_b, bc[r], bc_tail, r, cbw, cbb, slice(0, 128))
     pl.semaphore_wait(bar, len(others) + jnp.where(depth == 3, 4, 0))
 
-    def a2a(b, q):
+    def z_copy(s):
+        return rcopy(wsrc.at[s], wfar.at[s], z_send.at[s], z_recv.at[s], opposite)
+
+    def a2a(half, s, b, q):
+        source, d = ((wsrc, d_me), (wfar, d_far))[half]
         return rcopy(
-            wsrc.at[b, pl.ds(2 * q, 2)], wfull.at[d_me, pl.ds(2 * q, 2), x],
-            a2a_send.at[b, q], a2a_recv.at[x], at(x=2 * c + b, c=q),
+            source.at[s, b, q], wfull.at[d, 2 * q + s, x], a2a_send.at[half, s, b, q],
+            a2a_recv.at[half, s, x], at(x=2 * c + b, c=q),
         )
 
     def a2a_local(b, q):
         return jnp.logical_and(x == 2 * c + b, c == q)
 
-    for b in range(2):
-        for q in range(2):
-            @pl.when(jnp.logical_not(a2a_local(b, q)))
+    def a2a_start(half, s):
+        source, d = ((wsrc, d_me), (wfar, d_far))[half]
+        for b in range(2):
+            for q in range(2):
+                @pl.when(jnp.logical_not(a2a_local(b, q)))
+                def _():
+                    a2a(half, s, b, q).start()
+
+                @pl.when(a2a_local(b, q))
+                def _():
+                    wfull[d, 2 * q + s, x] = source[s, b, q]
+
+    def a2a_wait(half, s):
+        d = (d_me, d_far)[half]
+        for j in range(4):
+            @pl.when(jnp.logical_not(jnp.logical_and(x == j, c == x_owner)))
             def _():
-                a2a(b, q).start()
-
-            @pl.when(a2a_local(b, q))
-            def _():
-                wfull[d_me, 2 * q, x] = wsrc[b, 2 * q]
-                wfull[d_me, 2 * q + 1, x] = wsrc[b, 2 * q + 1]
+                slot = wfull.at[d, 2 * c + s, j]
+                rcopy(
+                    slot, slot, a2a_send.at[half, s, 0, 0], a2a_recv.at[half, s, j], sibling
+                ).wait_recv()
 
     def bc_copy(r, j):
         return rcopy(
             bcall.at[x, r], bcall.at[x, r], bc_send.at[r, j - 1], bc_recv.at[x, r], xn(j)
         )
 
-    for r in range(2):
+    def bc_start(r):
         for j in (1, 3, 2):
             bc_copy(r, j).start()
+
+    bc_start(0)
+    z_copy(0).start()
+    for s in range(2):
+        a2a_start(0, s)
 
     row = lax.broadcasted_iota(jnp.int32, (256, 256), 0)
     col = lax.broadcasted_iota(jnp.int32, (256, 256), 1)
@@ -237,43 +258,28 @@
         piece = wfull.at[d, 2 * c + s]
         return rcopy(piece, piece, y_send.at[half, s, j - 1], w_recv.at[d, s], yn(j))
 
-    def z_copy(s):
-        piece = wfull.at[d_me, 2 * c + s]
-        return rcopy(piece, piece, z_send.at[s], w_recv.at[d_me, s], opposite)
-
     def sib_copy(d, s):
         piece = wfull.at[d, 2 * c + s]
         return rcopy(piece, piece, sib_send.at[d, s], sib_recv.at[d, s], sibling)
 
     def w_wait(d, s):
         piece = wfull.at[d, 2 * c + s]
-        rcopy(piece, piece, z_send.at[s], w_recv.at[d, s], opposite).wait_recv()
+        rcopy(piece, piece, sib_send.at[d, s], w_recv.at[d, s], sibling).wait_recv()
 
     def sib_wait(d, s):
         piece = wfull.at[d, 2 * (1 - c) + s]
         rcopy(piece, piece, sib_send.at[d, s], sib_recv.at[d, s], sibling).wait_recv()
 
-    def spread_own():
-        for j in range(4):
-            @pl.when(jnp.logical_not(jnp.logical_and(x == j, c == x_owner)))
-            def _():
-                rcopy(
-                    wsrc.at[0, pl.ds(0, 2)], wfull.at[d_me, pl.ds(2 * c, 2), j],
-                    a2a_send.at[0, 0], a2a_recv.at[j], sibling,
-                ).wait_recv()
-
-        for s in range(2):
-            z_copy(s).start()
-        for s in range(2):
-            for j in (1, 3, 2):
-                y_copy(0, d_me, s, j).start()
-            sib_copy(d_me, s).start()
-
-    def spread_far(s):
-        w_wait(d_far, s)
+    def spread(half, s):
+        a2a_wait(half, s)
+        d = (d_me, d_far)[half]
         for j in (1, 3, 2):
-            y_copy(1, d_far, s, j).start()
-        sib_copy(d_far, s).start()
+            y_copy(half, d, s, j).start()
+        sib_copy(d, s).start()
+
+    def far_start(s):
+        z_copy(s).wait_recv()
+        a2a_start(1, s)
 
     def hand_over(half, s):
         for j in (1, 3, 2):
@@ -322,8 +328,9 @@
                 [wfull[d].reshape(2048, 128), wfull[d + 1].reshape(2048, 128)], axis=1
             )
             product = dot_nn(rows, both) * factor
-            part[r, d] = product[:, :128]
-            part[r, d + 1] = product[:, 128:]
+            for u in range(2):
+                part[2 * r + u, d] = product[u * 128:(u + 1) * 128, :128]
+                part[2 * r + u, d + 1] = product[u * 128:(u + 1) * 128, 128:]
 
     def s_copy(r, d, way, target):
         return rcopy(
@@ -357,7 +364,8 @@
                 d = half * 4 + spot + flip * (3 - 2 * spot)
                 way = (d < zl).astype(jnp.int32)
                 fed = seat_line + way * (3 - 2 * seat_line) > 0
-                relay(r, d, fed, way, way, zl + 1 - 2 * way)
+                for u in range(2):
+                    relay(2 * r + u, d, fed, way, way, zl + 1 - 2 * way)
                 return carry_
 
             lax.fori_loop(0, 3, body, 0)
@@ -368,7 +376,8 @@
                 d = half * 4 + i + half * (3 - 2 * i)
                 last = depth == 3
                 target = jnp.where(last, d, zl + 1 - 2 * half_line)
-                relay(r, d, depth > 0, 0, jnp.where(last, 2, 0), target)
+                for u in range(2):
+                    relay(2 * r + u, d, depth > 0, 0, jnp.where(last, 2, 0), target)
                 return carry_
 
             lax.fori_loop(0, 4, body, 0)
@@ -385,41 +394,51 @@
             part[r, zl] = part[r, zl] + rbuf[1, r, zl].astype(F32)
 
         s_wait(r, zl, 2)
-        out[r] = (part[r, zl] + rbuf[2, r, zl].astype(F32)).astype(BF16)
+        out[r // 2, r % 2 * 128:r % 2 * 128 + 128] = (
+            part[r, zl] + rbuf[2, r, zl].astype(F32)
+        ).astype(BF16)
 
     prepare(0)
-    spread_own()
+    bc_start(1)
     prepare(1)
     for i in (13, 1, 12):
         fetch(i).wait()
     bc_wait(0)
     ssd(0)
     g_start(0)
+    spread(0, 0)
+    spread(0, 1)
     bc_wait(1)
     ssd(1)
+    z_copy(0).wait_send()
+    z_copy(1).start()
+    far_start(0)
+    hand_over(zh, 0)
+    hand_over(zh, 1)
+    carry(0)
+    for j in (1, 2, 3):
+        g_copy(0, j).wait_send()
     g_start(1)
-    for s in range(2):
-        hand_over(zh, s)
-    carry(0)
+    spread(1, 0)
     carry(1)
-    spread_far(0)
     sib_all(zh)
+    far_start(1)
     g_wait(0)
     project(0, zh)
     relay_all(0, zh)
+    spread(1, 1)
+    hand_over(1 - zh, 0)
     g_wait(1)
     project(1, zh)
     relay_all(1, zh)
-    hand_over(1 - zh, 0)
-    spread_far(1)
     hand_over(1 - zh, 1)
     sib_all(1 - zh)
     project(0, 1 - zh)
     relay_all(0, 1 - zh)
     project(1, 1 - zh)
     relay_all(1, 1 - zh)
-    finish(0)
-    finish(1)
+    for r in range(4):
+        finish(r)
 
     for r in range(2):
         state_copy(r).wait()
@@ -427,9 +446,12 @@
         for q in range(2):
             @pl.when(jnp.logical_not(a2a_local(b, q)))
             def _():
-                a2a(b, q).wait_send()
+                for half in range(2):
+                    for s in range(2):
+                        a2a(half, s, b, q).wait_send()
     for s in range(2):
-        z_copy(s).wait_send()
+        if s == 1:
+            z_copy(s).wait_send()
         for j in (1, 2, 3):
             y_copy(0, d_me, s, j).wait_send()
             y_copy(1, d_far, s, j).wait_send()
@@ -438,7 +460,9 @@
     for r in range(2):
         for j in (1, 2, 3):
             bc_copy(r, j).wait_send()
-            g_copy(r, j).wait_send()
+            if r == 1:
+                g_copy(r, j).wait_send()
+    for r in range(4):
         for d in range(8):
             @pl.when(d != zl)
             def _():
@@ -469,7 +493,8 @@
         in_specs=[stay] * 17,
         out_specs=(vmem, stay),
         scratch_shapes=[pltpu.VMEM(a.shape, a.dtype) for a in operands] + [
-            pltpu.VMEM((2, 4, 128, 128), BF16),
+            pltpu.VMEM((2, 2, 2, 128, 128), BF16),
+            pltpu.VMEM((2, 2, 2, 128, 128), BF16),
             pltpu.VMEM((8, 4, 4, 128, 128), BF16),
             pltpu.VMEM((4, 2, 256, 128), BF16),
             pltpu.VMEM((2, 4, 4, 256, 128), BF16),
@@ -481,15 +506,16 @@
             pltpu.VMEM((2, 8, 256), F32),
             pltpu.VMEM((2, 8, 256), F32),
             pltpu.VMEM((256, 256), F32),
-            pltpu.VMEM((2, 8, 256, 128), F32),
-            pltpu.VMEM((2, 8, 256, 128), BF16),
-            pltpu.VMEM((3, 2, 8, 256, 128), BF16),
+            pltpu.VMEM((4, 8, 128, 128), F32),
+            pltpu.VMEM((4, 8, 128, 128), BF16),
+            pltpu.VMEM((3, 4, 8, 128, 128), BF16),
             pltpu.VMEM((2, 8, 64, 256), F32),
             dma((17,)),
             dma((2,)),
-            dma((2, 2)),
-            dma((4,)),
+            dma((2, 2, 2, 2)),
+            dma((2, 2, 4)),
             dma((2, 2, 3)),
+            dma((2,)),
             dma((2,)),
             dma((8, 2)),
             dma((8, 2)),
@@ -498,8 +524,8 @@
             dma((4, 2)),
             dma((2, 3)),
             dma((2, 4)),
-            dma((2, 8)),
-            dma((3, 2, 8)),
+            dma((4, 8)),
+            dma((3, 4, 8)),
         ],
         compiler_params=pltpu.CompilerParams(
             collective_id=0, has_side_effects=True, vmem_limit_bytes=60 * 1024 * 1024

time: 95.3 us -> 93.2 us (0.978)
  Pallas kernels: 90.6 us -> 88.5 us
    pallas_call x1, Pallas kernels: 90.6 us -> 88.5 us  [per_device(): pl.pallas_call(kernel, name='mixer', out_shape=(jax.ShapeDtypeStruct((2,...]
where the time goes in v3:
time: 93.2 us; the launch traced here: 93 us
  Pallas kernels  88.5 us (95%)
  local copies, waits for them, and re-layouts  3.86 us (4%)
    pallas_call x1, Pallas kernels, per_device(): pl.pallas_call(kernel, name='mixer', out_shape=(jax.ShapeDtypeStruct((2,...  88.5 us
    unnamed x2, local copies, waits for them, and re-layouts  3.86 us

profile of v3, /device:TPU:129, one launch (start us, length us, event | category | flops | bytes accessed | tf_op | source)
XLA Modules:
  0.0 93.0 jit_solution(13386469615522045800)
XLA Ops:
  0.6 88.5 %mixer.1 = (bf16[2,256,128]{2,1,0:T(8,128)(2,1)}, f32[2,8,64,256]{3,2,1,0:T(8,128)}) custom-call(bf16[2,256,512]{2,1,0:T(8,128)(2,1)} %bitcast.14, bf16[2,256,512]{2,1,0:T(8,128)(2,1)} %bitcast.15, bf16[2,256,128]{2,1,0:T(8,128)(2,1)} %bitcast.16, f32[8,512]{1,0:T(8,128)} %bitcast.18, bf16[3,2,512]{2,1,0:T(2,128)(2,1)} %bitcast.19, ...), custom_call_target="tpu_custom_call" | custom-call | tf_op jit(solution)/shard_map/mixer/pallas_call | solution.py:486
  89.1 1.6 %copy.21 = bf16[512,128]{1,0:T(8,128)(2,1)} copy(bf16[512,128]{1,0:T(8,128)(2,1)} %bitcast.17) | data formatting | bytes 262144
  90.7 2.3 %copy.22 = f32[2,8,64,256]{3,2,1,0:T(8,128)} copy(f32[2,8,64,256]{3,2,1,0:T(8,128)} %get-tuple-element.9) | data formatting | bytes 2097152

commit v4 on v3

--- a/solution.py
+++ b/solution.py
@@ -273,7 +273,7 @@
     def spread(half, s):
         a2a_wait(half, s)
         d = (d_me, d_far)[half]
-        for j in (1, 3, 2):
+        for j in (2, 1, 3):
             y_copy(half, d, s, j).start()
         sib_copy(d, s).start()
 
@@ -296,7 +296,7 @@
         return rcopy(gall.at[r, x], gall.at[r, x], g_send.at[r, j - 1], g_recv.at[r, x], xn(j))
 
     def g_start(r):
-        for j in (1, 3, 2):
+        for j in (2, 1, 3):
             g_copy(r, j).start()
 
     def g_wait(r):

time: 93.2 us -> 96.4 us (1.034)
  Pallas kernels: 88.5 us -> 91.5 us
    pallas_call x1, Pallas kernels: 88.5 us -> 91.5 us  [per_device(): pl.pallas_call(kernel, name='mixer', out_shape=(jax.ShapeDtypeStruct((2,...]
where the time goes in v4:
time: 96.4 us; the launch traced here: 96 us
  Pallas kernels  91.5 us (95%)
  local copies, waits for them, and re-layouts  3.86 us (4%)
    pallas_call x1, Pallas kernels, per_device(): pl.pallas_call(kernel, name='mixer', out_shape=(jax.ShapeDtypeStruct((2,...  91.5 us
    unnamed x2, local copies, waits for them, and re-layouts  3.86 us

profile of v4, /device:TPU:129, one launch (start us, length us, event | category | flops | bytes accessed | tf_op | source)
XLA Modules:
  0.0 96.0 jit_solution(3394460183702849035)
XLA Ops:
  0.6 91.5 %mixer.1 = (bf16[2,256,128]{2,1,0:T(8,128)(2,1)}, f32[2,8,64,256]{3,2,1,0:T(8,128)}) custom-call(bf16[2,256,512]{2,1,0:T(8,128)(2,1)} %bitcast.14, bf16[2,256,512]{2,1,0:T(8,128)(2,1)} %bitcast.15, bf16[2,256,128]{2,1,0:T(8,128)(2,1)} %bitcast.16, f32[8,512]{1,0:T(8,128)} %bitcast.18, bf16[3,2,512]{2,1,0:T(2,128)(2,1)} %bitcast.19, ...), custom_call_target="tpu_custom_call" | custom-call | tf_op jit(solution)/shard_map/mixer/pallas_call | solution.py:486
  92.1 1.6 %copy.21 = bf16[512,128]{1,0:T(8,128)(2,1)} copy(bf16[512,128]{1,0:T(8,128)(2,1)} %bitcast.17) | data formatting | bytes 262144
  93.7 2.3 %copy.22 = f32[2,8,64,256]{3,2,1,0:T(8,128)} copy(f32[2,8,64,256]{3,2,1,0:T(8,128)} %get-tuple-element.9) | data formatting | bytes 2097152
